TPU v7x, 512 devices: a whole 4x8x8 slice. The times are simulated.
512 devices in a mesh: row: 32 (over x, z_hi, core), col: 16 (over z_lo, y).
Axes of the slice: x: 4, y: 8, z: 8 (z_hi: 4, z_lo: 2; z = z_hi * 2 + z_lo), core: 2. Of those that a mesh axis runs over, the one named last changes fastest.
Arguments:
- embeddings: bfloat16 [65536, 128], P(('col', 'row')), may hold values from -6 to 6
- weight: bfloat16 [128, 256], replicated, may hold values from -0.5 to 0.5
- cotangent: bfloat16 [65536, 256], P(('row', 'col')), may hold values from -6 to 6
- adj_blocks: bfloat16 [32, 512, 4, 128, 128], P('row', 'col'), may hold values from -0.0625 to 0.0625
- block_rows: int32 [32, 512, 4], P('row', 'col'), may hold values from 0 to 15
- block_counts: int32 [32, 512], P('row', 'col'), may hold values from 0 to 4, as said below
Outputs:
- grad_embeddings: bfloat16 [65536, 128], P(('col', 'row'))
- grad_weight: float32 [128, 256], replicated
Inputs may be any that keep to these rules, and one draw needn't show every extreme that they name: `block_counts`: counts differ from tile to tile; the first block column of each tile carries that tile's largest count, and some tile reaches 4.
All inputs are finite; a program needn't handle non-finite values.
Results may differ from a plain program's by a relative error of at most 0.02.
Values may be sent and summed in bfloat16 or wider, within the bound.
A program may use at most 64 MiB of HBM per device.

v0:
```python
import jax
import jax.numpy as jnp
from jax import lax
from jax.sharding import PartitionSpec as P

BR = 16


def silu_slope(z):
    s = jax.nn.sigmoid(z)
    return s * (1.0 + z * (1.0 - s))


def body(embeddings, weight, cotangent, adj_blocks, block_rows, block_counts):
    blocks = adj_blocks[0]
    rows = block_rows[0]
    counts = block_counts[0]
    slots = blocks.shape[1]
    width = blocks.shape[2]
    feat = embeddings.shape[1]
    live = jnp.arange(slots, dtype=jnp.int32)[None, :] < counts[:, None]
    select = (
        (rows[:, :, None] == jnp.arange(BR, dtype=jnp.int32)[None, None, :]) & live[:, :, None]
    ).astype(jnp.float32)
    column_panel = lax.all_gather(embeddings, "row", axis=0, tiled=True)
    number = column_panel.shape[0] // width
    part = blocks
    picked = select
    prod = jnp.einsum(
        "jsab,jbf->jsaf",
        part,
        column_panel.reshape(number, width, feat),
        preferred_element_type=jnp.float32,
    )
    partial_rows = jnp.einsum("jsk,jsaf->kaf", picked, prod, precision=lax.Precision.HIGHEST)
    flat_rows = partial_rows.reshape(BR * width, feat)
    summed = lax.psum_scatter(flat_rows, "col", scatter_dimension=0, tiled=True)
    aggregate = summed.astype(jnp.bfloat16)
    pre = jnp.dot(aggregate, weight, preferred_element_type=jnp.float32)
    dpre = (cotangent.astype(jnp.float32) * silu_slope(pre)).astype(jnp.bfloat16)
    local_weight = jnp.dot(aggregate.T, dpre, preferred_element_type=jnp.float32)
    dagg = jnp.dot(dpre, weight.T, preferred_element_type=jnp.float32).astype(jnp.bfloat16)
    gathered = lax.all_gather(dagg, "col", axis=0, tiled=True).reshape(BR, width, feat)
    grad_weight = lax.psum(local_weight, ("row", "col"))
    chosen = jnp.take(gathered, rows, axis=0) * live[:, :, None, None].astype(jnp.bfloat16)
    count = lax.axis_size("row") * embeddings.shape[0]
    part = blocks
    picked = chosen
    terms = jnp.einsum("jsba,jsbf->jaf", part, picked, preferred_element_type=jnp.float32)
    grad_rows = lax.psum_scatter(
        terms.reshape(count, feat).astype(jnp.bfloat16), "row", scatter_dimension=0, tiled=True
    )
    return (grad_rows, grad_weight)


def solution(mesh):
    return jax.shard_map(
        body,
        mesh=mesh,
        in_specs=(
            P(("col", "row"), None),
            P(),
            P(("row", "col"), None),
            P("row", "col", None, None, None),
            P("row", "col", None),
            P("row", "col"),
        ),
        out_specs=(P(("col", "row"), None), P()),
        check_vma=False,
    )
```

profile of v0, /device:TPU:1, one launch (start us, length us, event | category | flops | bytes accessed | tf_op | source)
XLA Modules:
  0.0 525.9 jit_solution(16659653454605090907)
XLA Ops:
  7.2 0.0 copy-start
  7.2 0.0 all-gather.2.cloned.1.call-start
  7.2 0.7 all-gather.2.cloned.1.call-update
  7.9 0.0 reduce-scatter.3.cloned.1.call-start
  8.0 0.7 fusion.30
  8.6 66.5 %all-gather.2.cloned.1.call-done = bf16[4096,128]{1,0:T(8,128)(2,1)} async-done(((bf16[128,128]{1,0:T(8,128)(2,1)}), bf16[4096,128]{1,0:T(8,128)(2,1)}) %all-gather.2.cloned.1.call-update) | async-done | bytes 1048592 | tf_op jit(solution)/shard_map/all_gather | solution.py:25
  75.1 0.0 copy-start.1
  75.1 3.7 fusion.4
  78.8 0.0 copy-done.1
  78.8 0.0 copy-start.2
  78.9 7.8 %fusion.15 = f32[16,128,128]{2,0,1:T(8,128)S(1)} fusion(f32[32,4,128,128]{3,2,1,0:T(8,128)S(1)} %fusion.4, s32[32,4]{0,1:T(4,128)S(1)} %bitcast.44, pred[32,4]{0,1:T(4,128)(4,1)S(1)} %get-tuple-element.3), kind=kOutput, calls=%fused_computation.13 | convolution fusion | flops 402657280 | bytes 9437824 | tf_op jit(solution)/shard_map/jsk,jsaf->kaf/dot_general | solution.py:35
  86.6 1.3 copy.19
  87.9 0.0 reduce-scatter.3.cloned.1.call-update
  87.9 0.0 all-reduce.2.cloned.1.call-start
  88.0 0.1 copy.20
  88.1 0.1 reshape.104
  88.2 0.1 copy.21
  88.3 0.1 copy.17
  88.4 59.1 %reduce-scatter.3.cloned.1.call-done = f32[128,128]{1,0:T(8,128)} async-done(((f32[2048,128]{1,0:T(8,128)}), f32[128,128]{1,0:T(8,128)}) %reduce-scatter.3.cloned.1.call-update) | async-done | bytes 65552 | tf_op jit(solution)/shard_map/reduce_scatter | solution.py:37
  147.5 0.0 copy-done
  147.5 0.0 copy-done.2
  147.5 1.0 multiply_convert_fusion
  148.5 0.2 convolution_convert_fusion
  148.7 1.7 fusion.21
  150.4 0.0 all-reduce.2.cloned.1.call-update
  150.4 0.0 reduce-scatter.5.cloned.1.call-start
  150.5 27.4 %all_gather.7 = bf16[2048,128]{1,0:T(8,128)(2,1)S(1)} all-gather(bf16[128,128]{1,0:T(8,128)(2,1)S(1)} %convolution_convert_fusion), channel_id=1, replica_groups=mesh['row'=32,'col'=16] {'col'}, dimensions={0}, use_global_device_ids=true | all-gather | bytes 557056 | tf_op jit(solution)/shard_map/all_gather | solution.py:43
  177.9 3.0 gather_fusion
  180.9 6.3 %bitcast_convert_fusion = bf16[32,128,128]{1,2,0:T(8,128)(2,1)} fusion(bf16[1,32,4,128,128]{4,3,2,1,0:T(8,128)(2,1)} %param.9, bf16[32,4,128,128]{3,2,1,0:T(8,128)(2,1)} %bitcast.40, pred[32,4]{1,0:T(8,128)(4,1)S(1)} %copy.17, bf16[32,4]{1,0:T(8,128)(2,1)S(1)} %copy.21), kind=kOutput, calls=%fused_computation.10 | convolution fusion | flops 541589504 | bytes 9437568 | tf_op jit(solution)/shard_map/jsba,jsbf->jaf/dot_general | solution.py:49
  187.2 0.0 reduce-scatter.5.cloned.1.call-update
  187.2 236.4 %all-reduce.2.cloned.1.call-done = f32[128,256]{1,0:T(8,128)} async-done(((f32[128,256]{1,0:T(8,128)}), f32[128,256]{1,0:T(8,128)}) %all-reduce.2.cloned.1.call-update) | async-done | bytes 131088 | tf_op jit(solution)/shard_map/psum | solution.py:44
  423.6 94.2 %reduce-scatter.5.cloned.1.call-done = bf16[128,128]{1,0:T(8,128)(2,1)} async-done(((bf16[4096,128]{1,0:T(8,128)(2,1)}), bf16[128,128]{1,0:T(8,128)(2,1)}) %reduce-scatter.5.cloned.1.call-update) | async-done | bytes 32784 | tf_op jit(solution)/shard_map/reduce_scatter | solution.py:50
  517.8 1.6 copy.32
  (3 shorter events, 0.0 us)
Async XLA Ops:
  7.2 140.3 %copy-start = (bf16[128,256]{1,0:T(8,128)(2,1)S(1)}, bf16[128,256]{1,0:T(8,128)(2,1)}, u32[]{:S(2)}) copy-start(bf16[128,256]{1,0:T(8,128)(2,1)} %param.7) | copy-start | bytes 196612
  7.2 67.9 %all-gather.2.cloned.1.call-start = ((), (), s32[]{:S(2)}) async-start(), calls=%async_computation.2 | async-start | bytes 1081344 | tf_op jit(solution)/shard_map/all_gather | solution.py:25
  7.9 139.6 %reduce-scatter.3.cloned.1.call-start = ((), (), s32[]{:S(2)}) async-start(), calls=%async_computation.3 | async-start | bytes 1114112 | tf_op jit(solution)/shard_map/reduce_scatter | solution.py:37
  75.1 3.7 copy-start.1
  78.8 68.6 %copy-start.2 = (bf16[128,256]{1,0:T(8,128)(2,1)S(1)}, bf16[128,256]{1,0:T(8,128)(2,1)}, u32[]{:S(2)}) copy-start(bf16[128,256]{1,0:T(8,128)(2,1)} %param.8) | copy-start | bytes 196612
  87.9 335.7 %all-reduce.2.cloned.1.call-start = ((), (), s32[]{:S(2)}) async-start(), calls=%async_computation.5 | async-start | bytes 262144 | tf_op jit(solution)/shard_map/psum | solution.py:44
  150.4 367.4 %reduce-scatter.5.cloned.1.call-start = ((), (), s32[]{:S(2)}) async-start(), calls=%async_computation.4 | async-start | bytes 1081344 | tf_op jit(solution)/shard_map/reduce_scatter | solution.py:50
Sparse Core Ops, SparseCore 0:
  11.1 63.9 all-gather.1
  88.1 59.3 reduce-scatter.2
  153.8 269.7 all-reduce.1
  428.4 89.3 reduce-scatter.4
where the time goes:
time: 527 us; the launch traced here: 526 us
  waiting for transfers between devices  457 us (87%)
  blocking collectives  27.4 us (5%)
  matrix products  20.6 us (4%)
  between operations  13.8 us (3%)
  local copies, waits for them, and re-layouts  6.3 us (1%)
    psum x1, waiting for transfers between devices, body(): grad_weight = lax.psum(local_weight, ('row', 'col'))  236 us
    reduce_scatter x1, waiting for transfers between devices, body(): lax.psum_scatter(terms.reshape(count, feat).astype(jnp.bfloat16), 'row',...  94.2 us
    all_gather x1, waiting for transfers between devices, body(): column_panel = lax.all_gather(embeddings, 'row', axis=0, tiled=True)  66.5 us
    reduce_scatter x1, waiting for transfers between devices, body(): summed = lax.psum_scatter(flat_rows, 'col', scatter_dimension=0, tiled=True)  59.1 us
    all_gather x1, blocking collectives, body(): lax.all_gather(dagg, 'col', axis=0, tiled=True).reshape(BR, width, feat)  27.4 us
  transfers between devices with their start and end apart: 4, of which 4 were waited for; matrix products, arithmetic and copies ran while one was open for 2% of the time, Pallas kernels for 0%

commit v1 on v0

v1 whole, which is shorter than its diff:
```python
import functools

import jax
import jax.numpy as jnp
from jax import lax
from jax.experimental import pallas as pl
from jax.experimental.pallas import tpu as pltpu
from jax.sharding import PartitionSpec as P

MESH = pl.DeviceIdType.MESH
BR = 16
NX, NZ, NY, NC = 4, 4, 8, 32
SLOTS = 4
B = 128
F = 128
HID = 256
NB = NC * SLOTS
BF = jnp.bfloat16
F32 = jnp.float32


def ring4(t):
    return 1 + 2 * t - 3 * (t // 2)


def kernel(
    idx, emb, wgt, cot, adj_hbm, gout, gw_out,
    adj, panel, prod, seg, zs, zr, ys, yr, dt, gt, cs, cr, keep, xs, xr, hs, hr,
    lw, lwr, ws, wr, w1, w1r, w2, w2r, w3, w3r, wg,
    sem_a, e_s, e_r, z_s, z_r, y_s, y_r, g_s, g_r, c_s, c_r, x_s, x_r, h_s, h_r,
    w_s, w_r,
):
    row = lax.axis_index("row")
    col = lax.axis_index("col")
    x, zh, core = row // 8, (row // 2) % NZ, row % 2
    zl, y = col // NY, col % NY

    def to_x(d):
        return ((((x + d) % NX) * NZ + zh) * 2 + core, col)

    def to_h(d):
        return ((x * NZ + (zh + d) % NZ) * 2 + core, col)

    def to_y(d):
        return (row, zl * NY + (y + d) % NY)

    sib = ((x * NZ + zh) * 2 + 1 - core, col)
    mate = (row, (1 - zl) * NY + y)

    def node(dx, dz, c):
        return (((x + dx) % NX) * NZ + (zh + dz) % NZ) * 2 + c

    def remote(src, dst, s, r, where):
        return pltpu.make_async_remote_copy(
            src_ref=src, dst_ref=dst, send_sem=s, recv_sem=r, device_id=where, device_id_type=MESH
        )

    loads = [
        pltpu.make_async_copy(adj_hbm.at[pl.ds(8 * q, 8)], adj.at[pl.ds(8 * q, 8)], sem_a.at[q])
        for q in range(4)
    ]
    for cp in loads:
        cp.start()

    barrier = pltpu.get_barrier_semaphore()
    peers = [sib, mate] + [to_x(d) for d in (1, 2, 3)] + [to_h(d) for d in (1, 2, 3)]
    peers += [to_y(d) for d in range(1, NY)]
    for peer in peers:
        pl.semaphore_signal(barrier, inc=1, device_id=peer, device_id_type=MESH)
    me = node(0, 0, core)
    gt[BR] = jnp.zeros((B, B), BF)
    seg[NB] = jnp.zeros((B, F), F32)
    panel[me] = emb[...]
    pl.semaphore_wait(barrier, len(peers))

    def spread(j, n, where, src=None):
        return remote(panel.at[j] if src is None else src, panel.at[j], e_s.at[n], e_r.at[j], where)

    for t, d in enumerate((1, 3, 2)):
        spread(me, t, to_h(d), emb).start()
    for t, d in enumerate((1, 3, 2)):
        spread(me, 3 + t, to_x(d), emb).start()
    spread(me, 6, sib, emb).start()

    def multiply(j):
        prod[pl.ds(j * SLOTS, SLOTS)] = jnp.dot(
            adj[j], panel[j], preferred_element_type=F32
        ).reshape(SLOTS, B, F)

    for cp in loads:
        cp.wait()
    multiply(me)

    def from_z(t, carry):
        j = node(0, ring4(t), core)
        spread(j, 0, sib).wait_recv()
        for q, d in enumerate((1, 3, 2)):
            spread(j, 7 + 4 * t + q, to_x(d)).start()
        spread(j, 7 + 4 * t + 3, sib).start()
        multiply(j)
        return carry

    lax.fori_loop(0, 3, from_z, 0)

    def from_x(t, carry):
        j = node(ring4(t % 3), (ring4(t // 3 - 1)) * jnp.minimum(t // 3, 1), core)
        spread(j, 0, sib).wait_recv()
        spread(j, 19 + t, sib).start()
        multiply(j)
        return carry

    lax.fori_loop(0, 12, from_x, 0)

    def from_sib(t, carry):
        j = node(t % NX, t // NX, 1 - core)
        spread(j, 0, sib).wait_recv()
        multiply(j)
        return carry

    lax.fori_loop(0, 16, from_sib, 0)

    def segment(i, total):
        total = prod[idx[i]] + total * idx[NB + i].astype(F32)
        seg[i] = total
        return total

    lax.fori_loop(0, NB, segment, jnp.zeros((B, F), F32))

    order = (4, 3, 5, 2, 6, 1, 7, 0)

    def part(half, d):
        return seg[idx[3 * NB + half * NY + (y + d) % NY]]

    def zcopy(d):
        return remote(zs.at[d], zr.at[d], z_s.at[d], z_r.at[d], mate)

    def ycopy(d):
        return remote(ys.at[d], yr.at[d], y_s.at[d], y_r.at[d], to_y(d))

    for d in order:
        zs[d] = part(1 - zl, d).astype(BF)
        zcopy(d).start()
    for d in order[:-1]:
        zcopy(d).wait_recv()
        ys[d] = (part(zl, d) + zr[d].astype(F32)).astype(BF)
        ycopy(d).start()
    zcopy(0).wait_recv()
    total = part(zl, 0) + zr[0].astype(F32)
    for d in (1, 7, 2, 6, 3, 5, 4):
        ycopy(d).wait_recv()
        total = total + yr[d].astype(F32)
    aggregate = total.astype(BF)

    weight = wgt[...]
    pre = jnp.dot(aggregate, weight, preferred_element_type=F32)
    s = 1.0 / (1.0 + jnp.exp(-pre))
    dpre = (cot[...].astype(F32) * (s * (1.0 + pre * (1.0 - s)))).astype(BF)
    dt[...] = lax.dot_general(
        weight, dpre, (((1,), (1,)), ((), ())), preferred_element_type=F32
    ).astype(BF)

    def share(k, n, where, src=None):
        return remote(gt.at[k] if src is None else src, gt.at[k], g_s.at[n], g_r.at[k], where)

    for d in order[:-1]:
        share(col, d, to_y(d), dt).start()
    share(col, 0, mate, dt).start()
    gt[col] = dt[...]

    lw[...] = lax.dot_general(
        aggregate, dpre, (((0,), (0,)), ((), ())), preferred_element_type=F32
    ).reshape(BR, 8, HID)
    w_first = remote(lw.at[pl.ds((1 - zl) * NY, NY)], lwr, w_s.at[0], w_r.at[0], mate)
    w_first.start()

    for d in (1, 7, 2, 6, 3, 5, 4):
        k = zl * NY + (y + d) % NY
        share(k, 0, mate).wait_recv()
        share(k, 7 + d, mate).start()

    w_first.wait_recv()

    def w_second(d):
        return remote(ws.at[d], wr.at[d], w_s.at[d], w_r.at[d], to_y(d))

    for d in range(1, NY):
        q = (y + d) % NY
        ws[d] = lw[zl * NY + q] + lwr[q]
        w_second(d).start()
    wtot = lw[zl * NY + y] + lwr[y]

    for d in (0, 1, 7, 2, 6, 3, 5, 4):
        share((1 - zl) * NY + (y + d) % NY, 0, mate).wait_recv()

    for d in range(1, NY):
        w_second(d).wait_recv()
        wtot = wtot + wr[d]
    w1[...] = wtot
    w_core = remote(w1, w1r, w_s.at[8], w_r.at[8], sib)
    w_core.start()

    def column_grad(j):
        picked = jnp.concatenate([gt[idx[2 * NB + j * SLOTS + q]] for q in range(SLOTS)], axis=1)
        return jnp.dot(picked, adj[j], preferred_element_type=F32)

    def ccopy(t):
        return remote(cs.at[t], cr.at[t], c_s.at[t], c_r.at[t], sib)

    def far(n):
        return (5 * n + 2 - (n // 2) * 8 + (n // 3) * 5) % 4

    def xcopy(t, d):
        return remote(xs.at[t], xr.at[t], x_s.at[t], x_r.at[t], to_x(d))

    def produce(dz, dx):
        t = dz * NX + dx
        cs[t] = column_grad(node(dx, dz, 1 - core)).astype(BF)
        ccopy(t).start()
        keep[t] = column_grad(node(dx, dz, core))

    def pass_on(dz, dx):
        t = dz * NX + dx
        ccopy(t).wait_recv()
        both = keep[t] + cr[t].astype(F32)
        if dx == 0:
            keep[t] = both
        else:
            xs[t] = both.astype(BF)
            xcopy(t, dx).start()

    steps = [(dz, dx) for dz in (2, 1, 3, 0) for dx in (2, 1, 3, 0)]
    lag = 4
    for n in range(len(steps) + lag):
        if n < len(steps):
            produce(*steps[n])
        if n >= lag:
            pass_on(*steps[n - lag])

    w_core.wait_recv()
    first = jnp.where(core == 0, w1[...], w1r[...])
    second = jnp.where(core == 0, w1r[...], w1[...])
    w2[...] = first + second

    def w_x(d):
        return remote(w2, w2r.at[x], w_s.at[8 + d], w_r.at[8 + (NX - d) % NX], to_x(d))

    def w_x_recv(d):
        return remote(w2, w2r.at[(x + d) % NX], w_s.at[8 + d], w_r.at[8 + d], to_x(d))

    w2r[x] = w2[...]
    for d in (1, 3, 2):
        w_x(d).start()

    def hcopy(dz):
        return remote(hs.at[dz], hr.at[dz], h_s.at[dz], h_r.at[dz], to_h(dz))

    def w_h(d):
        return remote(w3, w3r.at[zh], w_s.at[11 + d], w_r.at[11 + (NZ - d) % NZ], to_h(d))

    def w_h_recv(d):
        return remote(w3, w3r.at[(zh + d) % NZ], w_s.at[11 + d], w_r.at[11 + d], to_h(d))

    def over_x(dz):
        acc = keep[dz * NX]
        for dx in (1, 3, 2):
            xcopy(dz * NX + dx, dx).wait_recv()
            acc = acc + xr[dz * NX + dx].astype(F32)
        return acc

    for dz in (2, 1):
        hs[dz] = over_x(dz).astype(BF)
        hcopy(dz).start()
    for d in (1, 3, 2):
        w_x_recv(d).wait_recv()
    w3[...] = (w2r[0] + w2r[1]) + (w2r[2] + w2r[3])
    w3r[zh] = w3[...]
    for d in (1, 3, 2):
        w_h(d).start()
    hs[3] = over_x(3).astype(BF)
    hcopy(3).start()
    acc = over_x(0)

    for d in (1, 3, 2):
        w_h_recv(d).wait_recv()
    wg[col] = (w3r[0] + w3r[1]) + (w3r[2] + w3r[3])

    def w_y(d):
        return remote(wg.at[col], wg.at[col], w_s.at[14 + d], w_r.at[14 + (NY - d) % NY], to_y(d))

    def w_y_recv(d):
        k = zl * NY + (y + d) % NY
        return remote(wg.at[k], wg.at[k], w_s.at[14 + d], w_r.at[14 + d], to_y(d))

    for d in order[:-1]:
        w_y(d).start()

    for dz in (1, 3, 2):
        hcopy(dz).wait_recv()
        acc = acc + hr[dz].astype(F32)
    gout[...] = acc.T.astype(BF)

    for d in (1, 7, 2, 6, 3, 5, 4):
        w_y_recv(d).wait_recv()
    w_last = remote(
        wg.at[pl.ds(zl * NY, NY)], wg.at[pl.ds(zl * NY, NY)], w_s.at[22], w_r.at[22], mate
    )
    w_last.start()

    for n in range(31):
        spread(me, n, sib).wait_send()
    for d in range(NY):
        zcopy(d).wait_send()
        if d:
            ycopy(d).wait_send()
    for n in range(15):
        share(col, n, mate).wait_send()
    for t in range(16):
        ccopy(t).wait_send()
        if t % NX:
            xcopy(t, 1).wait_send()
    for dz in (1, 2, 3):
        hcopy(dz).wait_send()
    w_first.wait_send()
    for d in range(1, NY):
        w_second(d).wait_send()
        w_y(d).wait_send()
    w_core.wait_send()
    for d in (1, 2, 3):
        w_x(d).wait_send()
        w_h(d).wait_send()
    w_last.wait()
    gw_out[...] = wg[...].reshape(F, HID)


def plan(rows, counts):
    live = jnp.arange(SLOTS, dtype=jnp.int32)[None, :] < counts[:, None]
    key = jnp.where(live, rows, BR).reshape(NB)
    at = jnp.arange(NB, dtype=jnp.int32)
    same = (key[None, :] == key[:, None]) & (at[None, :] < at[:, None])
    rank = jnp.sum(((key[None, :] < key[:, None]) | same).astype(jnp.int32), axis=1)
    more = jnp.sum(same.astype(jnp.int32), axis=1) > 0
    hit = rank[:, None] == at[None, :]
    order = jnp.sum(jnp.where(hit, at[:, None], 0), axis=0)
    cont = jnp.sum((hit & more[:, None]).astype(jnp.int32), axis=0)
    ids = jnp.arange(BR, dtype=jnp.int32)
    upto = jnp.sum((key[None, :] <= ids[:, None]).astype(jnp.int32), axis=1)
    some = jnp.sum((key[None, :] == ids[:, None]).astype(jnp.int32), axis=1) > 0
    last = jnp.where(some, upto - 1, NB)
    return jnp.concatenate([order, cont, key, last])


def body(embeddings, weight, cotangent, adj_blocks, block_rows, block_counts):
    idx = plan(block_rows[0], block_counts[0])
    adj = adj_blocks.reshape(NC, SLOTS * B, B)
    v = pltpu.VMEM
    dma = pltpu.SemaphoreType.DMA
    vmem = pl.BlockSpec(memory_space=pltpu.VMEM)
    tile = (B, F)
    wt = (8, HID)
    return pl.pallas_call(
        kernel,
        out_shape=(
            jax.ShapeDtypeStruct((B, F), BF),
            jax.ShapeDtypeStruct((F, HID), F32),
        ),
        in_specs=[
            pl.BlockSpec(memory_space=pltpu.SMEM), vmem, vmem, vmem, pl.BlockSpec(memory_space=pl.ANY),
        ],
        out_specs=(vmem, vmem),
        scratch_shapes=[
            v((NC, SLOTS * B, B), BF),
            v((NC,) + tile, BF),
            v((NB,) + tile, F32),
            v((NB + 1,) + tile, F32),
            v((NY,) + tile, BF), v((NY,) + tile, BF),
            v((NY,) + tile, BF), v((NY,) + tile, BF),
            v(tile, BF),
            v((BR + 1,) + tile, BF),
            v((16,) + tile, BF), v((16,) + tile, BF),
            v((16,) + tile, F32),
            v((16,) + tile, BF), v((16,) + tile, BF),
            v((NZ,) + tile, BF), v((NZ,) + tile, BF),
            v((BR,) + wt, F32), v((NY,) + wt, F32),
            v((NY,) + wt, F32), v((NY,) + wt, F32),
            v(wt, F32), v(wt, F32),
            v(wt, F32), v((NX,) + wt, F32),
            v(wt, F32), v((NZ,) + wt, F32),
            v((BR,) + wt, F32),
            dma((4,)), dma((31,)), dma((NC,)),
            dma((NY,)), dma((NY,)), dma((NY,)), dma((NY,)),
            dma((15,)), dma((BR,)), dma((16,)), dma((16,)),
            dma((16,)), dma((16,)), dma((NZ,)), dma((NZ,)),
            dma((23,)), dma((23,)),
        ],
        compiler_params=pltpu.CompilerParams(
            collective_id=0, has_side_effects=True, vmem_limit_bytes=48 * 2**20
        ),
    )(idx, embeddings, weight, cotangent, adj)


def solution(mesh):
    return jax.shard_map(
        body,
        mesh=mesh,
        in_specs=(
            P(("col", "row"), None),
            P(),
            P(("row", "col"), None),
            P("row", "col", None, None, None),
            P("row", "col", None),
            P("row", "col"),
        ),
        out_specs=(P(("col", "row"), None), P()),
        check_vma=False,
    )
```

time: 527 us -> 86 us (0.16)
  the two profiles are of different devices: /device:TPU:1 before, /device:TPU:4 now
where the time goes in v1:
time: 86 us; the launch traced here: 85.6 us
  Pallas kernels  76.9 us (89%)
  local copies, waits for them, and re-layouts  6.87 us (8%)
  other arithmetic  1.17 us (1%)
    pallas_call x1, Pallas kernels, body(): pl.pallas_call(kernel, out_shape=(jax.ShapeDtypeStruct((B, F), BF), jax.S...  76.9 us
    unnamed x11, local copies, waits for them, and re-layouts  6.66 us

profile of v1, /device:TPU:4, one launch (start us, length us, event | category | flops | bytes accessed | tf_op | source)
XLA Modules:
  0.0 85.6 jit_solution(11851048445633257559)
XLA Ops:
  0.6 0.7 iota_compare_fusion.2
  1.4 0.1 lt.61
  1.5 0.8 copy.10
  2.2 0.1 squeeze.3
  2.4 0.2 convert_reduce_fusion.1
  2.6 0.1 select_reduce_fusion
  2.7 0.1 convert_reduce_fusion.3
  2.8 0.0 copy-start
  2.8 2.2 %copy-done = bf16[1,32,4,128,128]{4,3,2,1,0:T(8,128)(2,1)S(1)} copy-done((bf16[1,32,4,128,128]{4,3,2,1,0:T(8,128)(2,1)S(1)}, bf16[1,32,4,128,128]{4,3,2,1,0:T(8,128)(2,1)}, u32[]{:S(2)}) %copy-start) | copy-done | bytes 4194328
  5.0 0.0 copy-start.1
  5.0 0.8 copy-done.1
  5.8 0.0 copy-start.2
  5.8 0.8 copy-done.2
  6.7 0.0 copy-start.3
  6.7 0.8 copy-done.3
  7.4 76.9 %shard_map.77 = (bf16[128,128]{1,0:T(8,128)(2,1)S(1)}, f32[128,256]{1,0:T(8,128)S(1)}) custom-call(s32[400]{0:T(512)S(1)} %pad_add_fusion.idx, bf16[128,128]{1,0:T(8,128)(2,1)S(1)} %copy-done.3, bf16[128,256]{1,0:T(8,128)(2,1)S(1)} %copy-done.1, bf16[128,256]{1,0:T(8,128)(2,1)S(1)} %copy-done.2, bf16[32,512,128]{2,1,0:T(8,128)(2,1)S(1)} %bitcast.2), custom_call_target="tpu_custom_call" | custom-call | tf_op jit(solution)/shard_map/pallas_call | solution.py:360
  84.4 0.6 copy.13
  85.0 0.7 copy.14
  (4 shorter events, 0.0 us)
Async XLA Ops:
  2.8 2.2 %copy-start = (bf16[1,32,4,128,128]{4,3,2,1,0:T(8,128)(2,1)S(1)}, bf16[1,32,4,128,128]{4,3,2,1,0:T(8,128)(2,1)}, u32[]{:S(2)}) copy-start(bf16[1,32,4,128,128]{4,3,2,1,0:T(8,128)(2,1)} %param.9) | copy-start | bytes 12582916
  5.0 0.8 copy-start.1
  5.8 0.8 copy-start.2
  6.7 0.8 copy-start.3

commit v2 on v1

v2 whole, which is shorter than its diff:
```python
import functools

import jax
import jax.numpy as jnp
from jax import lax
from jax.experimental import pallas as pl
from jax.experimental.pallas import tpu as pltpu
from jax.sharding import PartitionSpec as P

MESH = pl.DeviceIdType.MESH
BR = 16
NX, NZ, NY, NC = 4, 4, 8, 32
SLOTS = 4
VMEM_LIMIT = 40 * 2**20
B = 128
F = 128
HID = 256
NB = NC * SLOTS
BF = jnp.bfloat16
F32 = jnp.float32


def ring4(t):
    return 1 + 2 * t - 3 * (t // 2)


def kernel(
    rows_hbm, counts_hbm, emb_hbm, wgt_hbm, cot_hbm, adj_hbm, gout, gw_out,
    rows_in, counts_in, wide, table, idx, emb, wgt, cot,
    adj, panel, prod, seg, zs, zr, ys, yr, dt, gt, cs, cr, keep, xs, xr, hs, hr,
    lw, lwr, ws, wr, w1, w1r, w2, w2r, w3, w3r, wg,
    sem_a, e_s, e_r, z_s, z_r, y_s, y_r, g_s, g_r, c_s, c_r, x_s, x_r, h_s, h_r,
    w_s, w_r,
):
    row = lax.axis_index("row")
    col = lax.axis_index("col")
    x, zh, core = row // 8, (row // 2) % NZ, row % 2
    zl, y = col // NY, col % NY

    def to_x(d):
        return ((((x + d) % NX) * NZ + zh) * 2 + core, col)

    def to_h(d):
        return ((x * NZ + (zh + d) % NZ) * 2 + core, col)

    def to_y(d):
        return (row, zl * NY + (y + d) % NY)

    sib = ((x * NZ + zh) * 2 + 1 - core, col)
    mate = (row, (1 - zl) * NY + y)

    def node(dx, dz, c):
        return (((x + dx) % NX) * NZ + (zh + dz) % NZ) * 2 + c

    pending = []

    def remote(src, dst, s, r, where):
        return pltpu.make_async_remote_copy(
            src_ref=src, dst_ref=dst, send_sem=s, recv_sem=r, device_id=where, device_id_type=MESH
        )

    def send(cp):
        cp.start()
        pending.append(cp)

    def finish():
        for cp in pending:
            cp.wait_send()

    own_in = pltpu.make_async_copy(emb_hbm, emb, sem_a.at[4])
    own_in.start()
    plan_in = [
        pltpu.make_async_copy(rows_hbm, rows_in, sem_a.at[8]),
        pltpu.make_async_copy(counts_hbm, counts_in, sem_a.at[9]),
    ]
    for cp in plan_in:
        cp.start()
    loads = [
        pltpu.make_async_copy(adj_hbm.at[pl.ds(8 * q, 8)], adj.at[pl.ds(8 * q, 8)], sem_a.at[q])
        for q in range(4)
    ]
    loads.append(pltpu.make_async_copy(wgt_hbm, wgt, sem_a.at[5]))
    loads.append(pltpu.make_async_copy(cot_hbm, cot, sem_a.at[6]))
    for cp in loads:
        cp.start()

    barrier = pltpu.get_barrier_semaphore()
    peers = [sib, mate] + [to_x(d) for d in (1, 2, 3)] + [to_h(d) for d in (1, 2, 3)]
    peers += [to_y(d) for d in range(1, NY)]
    for peer in peers:
        pl.semaphore_signal(barrier, inc=1, device_id=peer, device_id_type=MESH)
    me = node(0, 0, core)
    gt[BR] = jnp.zeros((B, B), BF)
    seg[NB] = jnp.zeros((B, F), F32)
    own_in.wait()
    pl.semaphore_wait(barrier, len(peers))

    def spread(j, n, where, src=None):
        return remote(panel.at[j] if src is None else src, panel.at[j], e_s.at[n], e_r.at[j], where)

    for t, d in enumerate((1, 3, 2)):
        send(spread(me, t, to_h(d), emb))
    for t, d in enumerate((1, 3, 2)):
        send(spread(me, 3 + t, to_x(d), emb))
    send(spread(me, 6, sib, emb))
    panel[me] = emb[...]

    for cp in plan_in:
        cp.wait()
    wide[...] = jnp.zeros((8, B), jnp.int32)
    wide[0:SLOTS, 0:NC] = rows_in[...]
    wide[SLOTS : SLOTS + 1, 0:NC] = counts_in[...]
    lane = lax.broadcasted_iota(jnp.int32, (1, B), 1)
    limit = wide[SLOTS : SLOTS + 1, :]
    key = jnp.zeros((1, B), jnp.int32)
    for q in range(SLOTS):
        mine = jnp.where(limit > q, wide[q : q + 1, :], BR)
        mine = jnp.where(lane < NC, mine, 0)
        key = key + (pltpu.roll(mine, q * NC, 1) if q else mine)
    key_r = jnp.broadcast_to(key, (B, B))
    key_c = key_r.T
    at_r = lax.broadcasted_iota(jnp.int32, (B, B), 1)
    at_c = lax.broadcasted_iota(jnp.int32, (B, B), 0)
    same = jnp.where((key_c == key_r) & (at_c < at_r), 1, 0)
    less = jnp.where(key_c < key_r, 1, 0)
    more = jnp.sum(same, axis=0, keepdims=True)
    rank = more + jnp.sum(less, axis=0, keepdims=True)
    code = rank * 2 + jnp.where(more > 0, 1, 0)
    code_c = jnp.broadcast_to(code, (B, B)).T
    hit = (code_c >> 1) == at_r
    place = (at_c & (NC - 1)) * SLOTS + (at_c >> 5)
    table[0:1, :] = jnp.sum(jnp.where(hit, place, 0), axis=0, keepdims=True)
    table[1:2, :] = jnp.sum(jnp.where(hit, code_c & 1, 0), axis=0, keepdims=True)
    table[2:3, :] = key
    upto = jnp.sum(jnp.where(key_c <= at_r, 1, 0), axis=0, keepdims=True)
    some = jnp.sum(jnp.where(key_c == at_r, 1, 0), axis=0, keepdims=True)
    table[3:4, :] = jnp.where(some > 0, upto - 1, NB)
    table[4:8, :] = jnp.zeros((4, B), jnp.int32)
    to_idx = pltpu.make_async_copy(table, idx, sem_a.at[7])
    to_idx.start()

    def multiply(j):
        prod[pl.ds(j * SLOTS, SLOTS)] = jnp.dot(
            adj[j], panel[j], preferred_element_type=F32
        ).reshape(SLOTS, B, F)

    for cp in loads:
        cp.wait()
    multiply(me)

    def from_z(t, carry):
        j = node(0, ring4(t), core)
        spread(j, 0, sib).wait_recv()
        for q, d in enumerate((1, 3, 2)):
            spread(j, 7 + 4 * t + q, to_x(d)).start()
        spread(j, 7 + 4 * t + 3, sib).start()
        multiply(j)
        return carry

    lax.fori_loop(0, 3, from_z, 0)

    def from_x(t, carry):
        j = node(ring4(t % 3), t // 3, core)
        spread(j, 0, sib).wait_recv()
        spread(j, 19 + t, sib).start()
        multiply(j)
        return carry

    lax.fori_loop(0, 12, from_x, 0)

    def from_sib(t, carry):
        j = node(t % NX, t // NX, 1 - core)
        spread(j, 0, sib).wait_recv()
        multiply(j)
        return carry

    lax.fori_loop(0, 16, from_sib, 0)
    pending += [spread(me, n, sib) for n in range(7, 31)]
    to_idx.wait()

    def segment(i, total):
        total = prod[idx[0, i]] + total * idx[1, i].astype(F32)
        seg[i] = total
        return total

    lax.fori_loop(0, NB, segment, jnp.zeros((B, F), F32))

    order = (4, 3, 5, 2, 6, 1, 7, 0)

    def part(half, d):
        return seg[idx[3, half * NY + (y + d) % NY]]

    def zcopy(d):
        return remote(zs.at[d], zr.at[d], z_s.at[d], z_r.at[d], mate)

    def ycopy(d):
        return remote(ys.at[d], yr.at[d], y_s.at[d], y_r.at[d], to_y(d))

    for d in order:
        zs[d] = part(1 - zl, d).astype(BF)
        send(zcopy(d))
    for d in order[:-1]:
        zcopy(d).wait_recv()
        ys[d] = (part(zl, d) + zr[d].astype(F32)).astype(BF)
        send(ycopy(d))
    zcopy(0).wait_recv()
    total = part(zl, 0) + zr[0].astype(F32)
    for d in (1, 7, 2, 6, 3, 5, 4):
        ycopy(d).wait_recv()
        total = total + yr[d].astype(F32)
    aggregate = total.astype(BF)

    weight = wgt[...]
    pre = jnp.dot(aggregate, weight, preferred_element_type=F32)
    s = 1.0 / (1.0 + jnp.exp(-pre))
    dpre = (cot[...].astype(F32) * (s * (1.0 + pre * (1.0 - s)))).astype(BF)
    dt[...] = lax.dot_general(
        weight, dpre, (((1,), (1,)), ((), ())), preferred_element_type=F32
    ).astype(BF)

    def share(k, n, where, src=None):
        return remote(gt.at[k] if src is None else src, gt.at[k], g_s.at[n], g_r.at[k], where)

    send(share(col, 0, mate, dt))
    for d in (1, 7, 2, 6, 3, 5, 4):
        send(share(col, d, to_y(d), dt))
    gt[col] = dt[...]

    lw[...] = lax.dot_general(
        aggregate, dpre, (((0,), (0,)), ((), ())), preferred_element_type=F32
    ).reshape(BR, 8, HID)
    w_first = remote(lw.at[pl.ds((1 - zl) * NY, NY)], lwr, w_s.at[0], w_r.at[0], mate)
    send(w_first)

    for d in (1, 7, 2, 6, 3, 5, 4):
        k = zl * NY + (y + d) % NY
        share(k, 0, mate).wait_recv()
        send(share(k, 7 + d, mate))

    w_first.wait_recv()

    def w_second(d):
        return remote(ws.at[d], wr.at[d], w_s.at[d], w_r.at[d], to_y(d))

    for d in range(1, NY):
        q = (y + d) % NY
        ws[d] = lw[zl * NY + q] + lwr[q]
        send(w_second(d))
    wtot = lw[zl * NY + y] + lwr[y]

    for d in (0, 1, 7, 2, 6, 3, 5, 4):
        share((1 - zl) * NY + (y + d) % NY, 0, mate).wait_recv()

    w_core = remote(w1, w1r, w_s.at[8], w_r.at[8], sib)

    def w_x(d):
        return remote(w2, w2r.at[x], w_s.at[8 + d], w_r.at[8 + (NX - d) % NX], to_x(d))

    def w_x_recv(d):
        return remote(w2, w2r.at[(x + d) % NX], w_s.at[8 + d], w_r.at[8 + d], to_x(d))

    def w_h(d):
        return remote(w3, w3r.at[zh], w_s.at[11 + d], w_r.at[11 + (NZ - d) % NZ], to_h(d))

    def w_h_recv(d):
        return remote(w3, w3r.at[(zh + d) % NZ], w_s.at[11 + d], w_r.at[11 + d], to_h(d))

    def w_to_core():
        acc = wtot
        for d in range(1, NY):
            w_second(d).wait_recv()
            acc = acc + wr[d]
        w1[...] = acc
        send(w_core)

    def w_to_x():
        w_core.wait_recv()
        first = jnp.where(core == 0, w1[...], w1r[...])
        second = jnp.where(core == 0, w1r[...], w1[...])
        w2[...] = first + second
        w2r[x] = w2[...]
        for d in (1, 3, 2):
            send(w_x(d))

    def w_to_h():
        for d in (1, 3, 2):
            w_x_recv(d).wait_recv()
        w3[...] = (w2r[0] + w2r[1]) + (w2r[2] + w2r[3])
        w3r[zh] = w3[...]
        for d in (1, 3, 2):
            send(w_h(d))

    between = {1: w_to_core, 4: w_to_x, 11: w_to_h}

    def column_grad(j):
        picked = jnp.concatenate([gt[idx[2, q * NC + j]] for q in range(SLOTS)], axis=1)
        return jnp.dot(picked, adj[j], preferred_element_type=F32)

    def ccopy(t):
        return remote(cs.at[t], cr.at[t], c_s.at[t], c_r.at[t], sib)

    def xcopy(t, d):
        return remote(xs.at[t], xr.at[t], x_s.at[t], x_r.at[t], to_x(d))

    def produce(dz, dx):
        t = dz * NX + dx
        cs[t] = column_grad(node(dx, dz, 1 - core)).astype(BF)
        send(ccopy(t))
        keep[t] = column_grad(node(dx, dz, core))

    def pass_on(dz, dx):
        t = dz * NX + dx
        ccopy(t).wait_recv()
        both = keep[t] + cr[t].astype(F32)
        if dx == 0:
            keep[t] = both
        else:
            xs[t] = both.astype(BF)
            send(xcopy(t, dx))

    steps = [(dz, dx) for dz in (2, 1, 3, 0) for dx in (2, 1, 3, 0)]
    lag = 4
    for n in range(len(steps) + lag):
        if n < len(steps):
            produce(*steps[n])
        if n >= lag:
            pass_on(*steps[n - lag])
        if n in between:
            between[n]()

    def hcopy(dz):
        return remote(hs.at[dz], hr.at[dz], h_s.at[dz], h_r.at[dz], to_h(dz))

    def over_x(dz):
        acc = keep[dz * NX]
        for dx in (1, 3, 2):
            xcopy(dz * NX + dx, dx).wait_recv()
            acc = acc + xr[dz * NX + dx].astype(F32)
        return acc

    for dz in (2, 1):
        hs[dz] = over_x(dz).astype(BF)
        send(hcopy(dz))
    hs[3] = over_x(3).astype(BF)
    send(hcopy(3))

    for d in (1, 3, 2):
        w_h_recv(d).wait_recv()
    wg[col] = (w3r[0] + w3r[1]) + (w3r[2] + w3r[3])

    def w_y(d):
        return remote(wg.at[col], wg.at[col], w_s.at[14 + d], w_r.at[14 + (NY - d) % NY], to_y(d))

    def w_y_recv(d):
        k = zl * NY + (y + d) % NY
        return remote(wg.at[k], wg.at[k], w_s.at[14 + d], w_r.at[14 + d], to_y(d))

    for d in order[:-1]:
        send(w_y(d))

    acc = over_x(0)
    for dz in (1, 3, 2):
        hcopy(dz).wait_recv()
        acc = acc + hr[dz].astype(F32)
    gout[...] = acc.T.astype(BF)

    for d in (1, 7, 2, 6, 3, 5, 4):
        w_y_recv(d).wait_recv()
    w_last = remote(
        wg.at[pl.ds(zl * NY, NY)], wg.at[pl.ds(zl * NY, NY)], w_s.at[22], w_r.at[22], mate
    )
    send(w_last)
    w_last.wait_recv()
    gw_out[...] = wg[...].reshape(F, HID)
    finish()


def body(embeddings, weight, cotangent, adj_blocks, block_rows, block_counts):
    adj = adj_blocks.reshape(NC, SLOTS * B, B)
    v = pltpu.VMEM
    dma = pltpu.SemaphoreType.DMA
    vmem = pl.BlockSpec(memory_space=pltpu.VMEM)
    hbm = pl.BlockSpec(memory_space=pltpu.HBM)
    tile = (B, F)
    wt = (8, HID)
    return pl.pallas_call(
        kernel,
        out_shape=(
            jax.ShapeDtypeStruct((B, F), BF),
            jax.ShapeDtypeStruct((F, HID), F32),
        ),
        in_specs=[hbm] * 6,
        out_specs=(vmem, vmem),
        scratch_shapes=[
            v((SLOTS, NC), jnp.int32), v((1, NC), jnp.int32),
            v((8, B), jnp.int32), v((8, B), jnp.int32),
            pltpu.SMEM((8, B), jnp.int32),
            v(tile, BF), v((F, HID), BF), v((B, HID), BF),
            v((NC, SLOTS * B, B), BF),
            v((NC,) + tile, BF),
            v((NB,) + tile, F32),
            v((NB + 1,) + tile, F32),
            v((NY,) + tile, BF), v((NY,) + tile, BF),
            v((NY,) + tile, BF), v((NY,) + tile, BF),
            v(tile, BF),
            v((BR + 1,) + tile, BF),
            v((16,) + tile, BF), v((16,) + tile, BF),
            v((16,) + tile, F32),
            v((16,) + tile, BF), v((16,) + tile, BF),
            v((NZ,) + tile, BF), v((NZ,) + tile, BF),
            v((BR,) + wt, F32), v((NY,) + wt, F32),
            v((NY,) + wt, F32), v((NY,) + wt, F32),
            v(wt, F32), v(wt, F32),
            v(wt, F32), v((NX,) + wt, F32),
            v(wt, F32), v((NZ,) + wt, F32),
            v((BR,) + wt, F32),
            dma((10,)), dma((31,)), dma((NC,)),
            dma((NY,)), dma((NY,)), dma((NY,)), dma((NY,)),
            dma((15,)), dma((BR,)), dma((16,)), dma((16,)),
            dma((16,)), dma((16,)), dma((NZ,)), dma((NZ,)),
            dma((23,)), dma((23,)),
        ],
        compiler_params=pltpu.CompilerParams(
            collective_id=0, has_side_effects=True, vmem_limit_bytes=VMEM_LIMIT
        ),
    )(*[
        pltpu.with_memory_space_constraint(a, pltpu.HBM)
        for a in (block_rows[0].T, block_counts, embeddings, weight, cotangent, adj)
    ])


def solution(mesh):
    return jax.shard_map(
        body,
        mesh=mesh,
        in_specs=(
            P(("col", "row"), None),
            P(),
            P(("row", "col"), None),
            P("row", "col", None, None, None),
            P("row", "col", None),
            P("row", "col"),
        ),
        out_specs=(P(("col", "row"), None), P()),
        check_vma=False,
    )
```

time: 86 us -> 75 us (0.87)
  the two profiles are of different devices: /device:TPU:4 before, /device:TPU:64 now
where the time goes in v2:
time: 75 us; the launch traced here: 74.9 us
  Pallas kernels  73 us (97%)
  local copies, waits for them, and re-layouts  1.27 us (2%)
    pallas_call x1, Pallas kernels, body(): pl.pallas_call(kernel, out_shape=(jax.ShapeDtypeStruct((B, F), BF), jax.S...  73 us

profile of v2, /device:TPU:64, one launch (start us, length us, event | category | flops | bytes accessed | tf_op | source)
XLA Modules:
  0.0 74.9 jit_solution(8410540154305673623)
XLA Ops:
  0.6 73.0 %shard_map.77 = (bf16[128,128]{1,0:T(8,128)(2,1)S(1)}, f32[128,256]{1,0:T(8,128)S(1)}) custom-call(s32[4,32]{1,0:T(4,128)} %bitcast.5, s32[1,32]{1,0:T(1,128)} %counts_hbm.1, bf16[128,128]{1,0:T(8,128)(2,1)} %emb_hbm.1, bf16[128,256]{1,0:T(8,128)(2,1)} %wgt_hbm.1, bf16[128,256]{1,0:T(8,128)(2,1)} %cot_hbm.1, bf16[32,512,128]{2,1,0:T(8,128)(2,1)} %bitcast.4), custom_call_target="tpu_custom_call" | custom-call | tf_op jit(solution)/shard_map/pallas_call | solution.py:386
  73.6 0.6 copy.10
  74.2 0.7 copy.11

commit v3 on v2

v3 whole, which is shorter than its diff:
```python
import functools

import jax
import jax.numpy as jnp
from jax import lax
from jax.experimental import pallas as pl
from jax.experimental.pallas import tpu as pltpu
from jax.sharding import PartitionSpec as P

MESH = pl.DeviceIdType.MESH
BR = 16
NX, NZ, NY, NC = 4, 4, 8, 32
SLOTS = 4
VMEM_LIMIT = 40 * 2**20
B = 128
F = 128
HID = 256
NB = NC * SLOTS
BF = jnp.bfloat16
F32 = jnp.float32


def ring4(t):
    return 1 + 2 * t - 3 * lax.div(t, 2)


def wrap(a, n):
    return lax.rem(a, n)


def kernel(
    rows_hbm, counts_hbm, emb_hbm, wgt_hbm, cot_hbm, adj_hbm, gout, gw_out,
    rows_in, counts_in, wide, table, idx, emb, wgt, cot,
    adj, panel, prod, seg, zs, zr, ys, yr, dt, gt, cs, cr, keep, xs, xr, hs, hr,
    lw, lr, ws, wr, pr, wg,
    sem_a, out, e_r, z_r, y_r, g_r, c_r, x_r, h_r, w_r,
):
    row = lax.axis_index("row")
    col = lax.axis_index("col")
    x, zh, core = lax.div(row, 8), wrap(lax.div(row, 2), NZ), wrap(row, 2)
    zl, y = lax.div(col, NY), wrap(col, NY)

    def to_x(d):
        return ((wrap(x + d, NX) * NZ + zh) * 2 + core, col)

    def to_h(d):
        return ((x * NZ + wrap(zh + d, NZ)) * 2 + core, col)

    def to_y(d):
        return (row, zl * NY + wrap(y + d, NY))

    sib = ((x * NZ + zh) * 2 + 1 - core, col)
    mate = (row, (1 - zl) * NY + y)

    def node(dx, dz, c):
        return (wrap(x + dx, NX) * NZ + wrap(zh + dz, NZ)) * 2 + c

    def remote(src, dst, s, r, where):
        return pltpu.make_async_remote_copy(
            src_ref=src, dst_ref=dst, send_sem=s, recv_sem=r, device_id=where, device_id_type=MESH
        )

    def send(cp):
        cp.start()

    def arrived(ref, sem):
        remote(ref, ref, out.at[0], sem, sib).wait_recv()

    def finish():
        groups = (
            panel.at[pl.ds(0, 31)], zs, ys.at[pl.ds(0, 7)], gt.at[pl.ds(0, 15)], cs,
            xs.at[pl.ds(0, 12)], hs.at[pl.ds(0, 3)], lw.at[0], ws.at[pl.ds(0, 15)],
            pr.at[pl.ds(0, 15)], wg.at[0, pl.ds(0, 15)], wg.at[0],
        )
        for n, ref in enumerate(groups):
            remote(ref, ref, out.at[n], out.at[n], sib).wait_send()

    own_in = pltpu.make_async_copy(emb_hbm, emb, sem_a.at[4])
    own_in.start()
    plan_in = [
        pltpu.make_async_copy(rows_hbm, rows_in, sem_a.at[8]),
        pltpu.make_async_copy(counts_hbm, counts_in, sem_a.at[9]),
    ]
    for cp in plan_in:
        cp.start()
    loads = [
        pltpu.make_async_copy(adj_hbm.at[pl.ds(8 * q, 8)], adj.at[pl.ds(8 * q, 8)], sem_a.at[q])
        for q in range(4)
    ]
    loads.append(pltpu.make_async_copy(wgt_hbm, wgt, sem_a.at[5]))
    loads.append(pltpu.make_async_copy(cot_hbm, cot, sem_a.at[6]))
    for cp in loads:
        cp.start()

    barrier = pltpu.get_barrier_semaphore()
    peers = [sib, mate] + [to_x(d) for d in (1, 2, 3)] + [to_h(d) for d in (1, 2, 3)]
    peers += [to_y(d) for d in range(1, NY)]
    for peer in peers:
        pl.semaphore_signal(barrier, inc=1, device_id=peer, device_id_type=MESH)
    me = node(0, 0, core)
    gt[BR] = jnp.zeros((B, B), BF)
    seg[NB] = jnp.zeros((B, F), F32)
    own_in.wait()
    pl.semaphore_wait(barrier, len(peers))

    def spread(j, where, src=None, sem=None):
        return remote(
            panel.at[j] if src is None else src, panel.at[j], out.at[0],
            e_r.at[j] if sem is None else sem, where,
        )

    for d in (1, 3, 2):
        send(spread(me, to_h(d), emb))
    for d in (1, 3, 2):
        send(spread(me, to_x(d), emb))
    send(spread(me, sib, emb, e_r.at[NC]))
    panel[me] = emb[...]

    for cp in plan_in:
        cp.wait()
    wide[...] = jnp.zeros((8, B), jnp.int32)
    wide[0:SLOTS, 0:NC] = rows_in[...]
    wide[SLOTS : SLOTS + 1, 0:NC] = counts_in[...]
    lane = lax.broadcasted_iota(jnp.int32, (1, B), 1)
    limit = wide[SLOTS : SLOTS + 1, :]
    key = jnp.zeros((1, B), jnp.int32)
    for q in range(SLOTS):
        mine = jnp.where(limit > q, wide[q : q + 1, :], BR)
        mine = jnp.where(lane < NC, mine, 0)
        key = key + (pltpu.roll(mine, q * NC, 1) if q else mine)
    key_r = jnp.broadcast_to(key, (B, B))
    key_c = key_r.T
    at_r = lax.broadcasted_iota(jnp.int32, (B, B), 1)
    at_c = lax.broadcasted_iota(jnp.int32, (B, B), 0)
    same = jnp.where((key_c == key_r) & (at_c < at_r), 1, 0)
    less = jnp.where(key_c < key_r, 1, 0)
    more = jnp.sum(same, axis=0, keepdims=True)
    rank = more + jnp.sum(less, axis=0, keepdims=True)
    code = rank * 2 + jnp.where(more > 0, 1, 0)
    code_c = jnp.broadcast_to(code, (B, B)).T
    hit = (code_c >> 1) == at_r
    place = (at_c & (NC - 1)) * SLOTS + (at_c >> 5)
    table[0:1, :] = jnp.sum(jnp.where(hit, place, 0), axis=0, keepdims=True)
    table[1:2, :] = jnp.sum(jnp.where(hit, code_c & 1, 0), axis=0, keepdims=True)
    table[2:3, :] = key
    upto = jnp.sum(jnp.where(key_c <= at_r, 1, 0), axis=0, keepdims=True)
    some = jnp.sum(jnp.where(key_c == at_r, 1, 0), axis=0, keepdims=True)
    table[3:4, :] = jnp.where(some > 0, upto - 1, NB)
    table[4:8, :] = jnp.zeros((4, B), jnp.int32)
    to_idx = pltpu.make_async_copy(table, idx, sem_a.at[7])
    to_idx.start()

    def multiply(j):
        prod[pl.ds(j * SLOTS, SLOTS)] = jnp.dot(
            adj[j], panel[j], preferred_element_type=F32
        ).reshape(SLOTS, B, F)

    for cp in loads:
        cp.wait()
    multiply(me)

    for dz in (1, 3, 2):
        j = node(0, dz, core)
        spread(j, sib).wait_recv()
        for d in (1, 3, 2):
            send(spread(j, to_x(d)))
        send(spread(j, sib, None, e_r.at[NC + dz]))
        multiply(j)

    def from_x(dz, t, carry):
        j = node(ring4(t), dz, core)
        spread(j, sib).wait_recv()
        send(spread(j, sib, None, e_r.at[NC + dz]))
        multiply(j)
        return carry

    def from_sib(dz, t, carry):
        multiply(node(t, dz, 1 - core))
        return carry

    for dz in (0, 1, 3, 2):
        lax.fori_loop(0, 3, functools.partial(from_x, dz), 0)
    for dz in (0, 1, 3, 2):
        arrived(panel.at[pl.ds(0, NX)], e_r.at[NC + dz])
        lax.fori_loop(0, NX, functools.partial(from_sib, dz), 0)
    to_idx.wait()

    def segment(i, total):
        total = prod[idx[0, i]] + total * idx[1, i].astype(F32)
        seg[i] = total
        return total

    lax.fori_loop(0, NB, segment, jnp.zeros((B, F), F32))

    order = (4, 3, 5, 2, 6, 1, 7, 0)

    def part(half, d):
        return seg[idx[3, half * NY + wrap(y + d, NY)]]

    def zcopy(d):
        return remote(zs.at[d], zr.at[d], out.at[1], z_r.at[d], mate)

    def ycopy(d):
        return remote(ys.at[d], yr.at[d], out.at[2], y_r.at[0], to_y(d))

    for d in order:
        zs[d] = part(1 - zl, d).astype(BF)
        send(zcopy(d))
    for d in order[:-1]:
        zcopy(d).wait_recv()
        ys[d] = (part(zl, d) + zr[d].astype(F32)).astype(BF)
        send(ycopy(d))
    zcopy(0).wait_recv()
    total = part(zl, 0) + zr[0].astype(F32)
    arrived(yr.at[pl.ds(1, NY - 1)], y_r.at[0])
    for d in range(1, NY):
        total = total + yr[d].astype(F32)
    aggregate = total.astype(BF)

    weight = wgt[...]
    pre = jnp.dot(aggregate, weight, preferred_element_type=F32)
    s = 1.0 / (1.0 + jnp.exp(-pre))
    dpre = (cot[...].astype(F32) * (s * (1.0 + pre * (1.0 - s)))).astype(BF)
    dt[...] = lax.dot_general(
        weight, dpre, (((1,), (1,)), ((), ())), preferred_element_type=F32
    ).astype(BF)

    def share(k, where, src=None, sem=None):
        return remote(
            gt.at[k] if src is None else src, gt.at[k], out.at[3],
            g_r.at[k] if sem is None else sem, where,
        )

    send(share(col, mate, dt, g_r.at[BR]))
    for d in (1, 7, 2, 6, 3, 5, 4):
        send(share(col, to_y(d), dt))
    gt[col] = dt[...]

    grad_w = lax.dot_general(
        aggregate, dpre, (((0,), (0,)), ((), ())), preferred_element_type=F32
    )
    for c in range(2):
        lw[c] = grad_w[:, c * 128 : (c + 1) * 128].reshape(BR, 8, 128)
    chip = lax.div(row, 2)

    def w_half():
        return remote(lw.at[1 - core], lr, out.at[7], w_r.at[0], sib)

    def w_to_col():
        arrived(lr, w_r.at[0])
        ws[...] = lw[core] + lr[...]
        for d in range(1, BR):
            k = wrap(col + d, BR)
            send(remote(ws.at[k], wr.at[col], out.at[8], w_r.at[1], (row, k)))
        wr[col] = ws[col]

    def w_to_plane():
        arrived(wr.at[pl.ds(0, 15)], w_r.at[1])
        pr[chip] = jnp.sum(wr[...], axis=0)
        for d in range(1, 16):
            q = wrap(chip + d, 16)
            send(remote(pr.at[chip], pr.at[chip], out.at[9], w_r.at[2], (q * 2 + core, col)))

    def w_from_plane():
        arrived(pr.at[pl.ds(0, 15)], w_r.at[2])
        wg[core, col] = jnp.sum(pr[...], axis=0)
        for d in range(1, BR):
            k = wrap(col + d, BR)
            send(remote(wg.at[core, col], wg.at[core, col], out.at[10], w_r.at[3], (row, k)))

    def w_last():
        return remote(wg.at[core], wg.at[core], out.at[11], w_r.at[4], sib)

    def w_to_sib():
        arrived(wg.at[core, pl.ds(0, 15)], w_r.at[3])
        send(w_last())

    send(w_half())
    for n, d in enumerate((1, 7, 2, 6, 3, 5, 4)):
        k = zl * NY + wrap(y + d, NY)
        share(k, mate).wait_recv()
        send(share(k, mate, None, g_r.at[BR]))
        if n == 1:
            w_to_col()

    arrived(gt.at[pl.ds(0, NY)], g_r.at[BR])
    w_to_plane()
    def column_grad(j):
        picked = jnp.concatenate([gt[idx[2, q * NC + j]] for q in range(SLOTS)], axis=1)
        return jnp.dot(picked, adj[j], preferred_element_type=F32)

    def ccopy(t):
        return remote(cs.at[t], cr.at[t], out.at[4], c_r.at[t], sib)

    def xcopy(t, d):
        return remote(xs.at[t], xr.at[t], out.at[5], x_r.at[t // NX], to_x(d))

    def produce(dz, dx):
        t = dz * NX + dx
        cs[t] = column_grad(node(dx, dz, 1 - core)).astype(BF)
        send(ccopy(t))
        keep[t] = column_grad(node(dx, dz, core))

    def pass_on(dz, dx):
        t = dz * NX + dx
        ccopy(t).wait_recv()
        both = keep[t] + cr[t].astype(F32)
        if dx == 0:
            keep[t] = both
        else:
            xs[t] = both.astype(BF)
            send(xcopy(t, dx))

    steps = [(dz, dx) for dz in (2, 1, 3, 0) for dx in (2, 1, 3, 0)]
    lag = 4
    for n in range(len(steps) + lag):
        if n < len(steps):
            produce(*steps[n])
        if n >= lag:
            pass_on(*steps[n - lag])
        if n == 10:
            w_from_plane()

    def hcopy(dz):
        return remote(hs.at[dz], hr.at[dz], out.at[6], h_r.at[0], to_h(dz))

    def over_x(dz):
        acc = keep[dz * NX]
        arrived(xr.at[pl.ds(dz * NX + 1, NX - 1)], x_r.at[dz])
        for dx in (1, 2, 3):
            acc = acc + xr[dz * NX + dx].astype(F32)
        return acc

    for dz in (2, 1):
        hs[dz] = over_x(dz).astype(BF)
        send(hcopy(dz))
    hs[3] = over_x(3).astype(BF)
    send(hcopy(3))

    w_to_sib()
    acc = over_x(0)
    arrived(hr.at[pl.ds(1, NZ - 1)], h_r.at[0])
    for dz in (1, 2, 3):
        acc = acc + hr[dz].astype(F32)
    gout[...] = acc.T.astype(BF)

    w_last().wait_recv()
    for c in range(2):
        gw_out[:, c * 128 : (c + 1) * 128] = wg[c].reshape(F, 128)
    finish()


def body(embeddings, weight, cotangent, adj_blocks, block_rows, block_counts):
    adj = adj_blocks.reshape(NC, SLOTS * B, B)
    v = pltpu.VMEM
    dma = pltpu.SemaphoreType.DMA
    vmem = pl.BlockSpec(memory_space=pltpu.VMEM)
    hbm = pl.BlockSpec(memory_space=pltpu.HBM)
    tile = (B, F)
    wt = (8, 128)
    return pl.pallas_call(
        kernel,
        out_shape=(
            jax.ShapeDtypeStruct((B, F), BF),
            jax.ShapeDtypeStruct((F, HID), F32),
        ),
        in_specs=[hbm] * 6,
        out_specs=(vmem, vmem),
        scratch_shapes=[
            v((SLOTS, NC), jnp.int32), v((1, NC), jnp.int32),
            v((8, B), jnp.int32), v((8, B), jnp.int32),
            pltpu.SMEM((8, B), jnp.int32),
            v(tile, BF), v((F, HID), BF), v((B, HID), BF),
            v((NC, SLOTS * B, B), BF),
            v((NC,) + tile, BF),
            v((NB,) + tile, F32),
            v((NB + 1,) + tile, F32),
            v((NY,) + tile, BF), v((NY,) + tile, BF),
            v((NY,) + tile, BF), v((NY,) + tile, BF),
            v(tile, BF),
            v((BR + 1,) + tile, BF),
            v((16,) + tile, BF), v((16,) + tile, BF),
            v((16,) + tile, F32),
            v((16,) + tile, BF), v((16,) + tile, BF),
            v((NZ,) + tile, BF), v((NZ,) + tile, BF),
            v((2, BR) + wt, F32), v((BR,) + wt, F32),
            v((BR,) + wt, F32), v((BR,) + wt, F32),
            v((16,) + wt, F32), v((2, BR) + wt, F32),
            dma((10,)), dma((12,)), dma((NC + NZ,)), dma((NY,)), dma((1,)), dma((BR + 1,)),
            dma((16,)), dma((NZ,)), dma((1,)), dma((5,)),
        ],
        compiler_params=pltpu.CompilerParams(
            collective_id=0, has_side_effects=True, vmem_limit_bytes=VMEM_LIMIT
        ),
    )(*[
        pltpu.with_memory_space_constraint(a, pltpu.HBM)
        for a in (block_rows[0].T, block_counts, embeddings, weight, cotangent, adj)
    ])


def solution(mesh):
    return jax.shard_map(
        body,
        mesh=mesh,
        in_specs=(
            P(("col", "row"), None),
            P(),
            P(("row", "col"), None),
            P("row", "col", None, None, None),
            P("row", "col", None),
            P("row", "col"),
        ),
        out_specs=(P(("col", "row"), None), P()),
        check_vma=False,
    )
```

time: 75 us -> 69.5 us (0.927)
  the two profiles are of different devices: /device:TPU:64 before, /device:TPU:1 now
where the time goes in v3:
time: 69.5 us; the launch traced here: 69.4 us
  Pallas kernels  67.5 us (97%)
  local copies, waits for them, and re-layouts  1.27 us (2%)
    pallas_call x1, Pallas kernels, body(): pl.pallas_call(kernel, out_shape=(jax.ShapeDtypeStruct((B, F), BF), jax.S...  67.5 us

profile of v3, /device:TPU:1, one launch (start us, length us, event | category | flops | bytes accessed | tf_op | source)
XLA Modules:
  0.0 69.4 jit_solution(14989668246675051359)
XLA Ops:
  0.6 67.5 %shard_map.77 = (bf16[128,128]{1,0:T(8,128)(2,1)S(1)}, f32[128,256]{1,0:T(8,128)S(1)}) custom-call(s32[4,32]{1,0:T(4,128)} %bitcast.5, s32[1,32]{1,0:T(1,128)} %counts_hbm.1, bf16[128,128]{1,0:T(8,128)(2,1)} %emb_hbm.1, bf16[128,256]{1,0:T(8,128)(2,1)} %wgt_hbm.1, bf16[128,256]{1,0:T(8,128)(2,1)} %cot_hbm.1, bf16[32,512,128]{2,1,0:T(8,128)(2,1)} %bitcast.4), custom_call_target="tpu_custom_call" | custom-call | tf_op jit(solution)/shard_map/pallas_call | solution.py:361
  68.1 0.6 copy.10
  68.7 0.7 copy.11

commit v4 on v3

--- a/solution.py
+++ b/solution.py
@@ -77,6 +77,11 @@
 
     own_in = pltpu.make_async_copy(emb_hbm, emb, sem_a.at[4])
     own_in.start()
+    barrier = pltpu.get_barrier_semaphore()
+    peers = [sib, mate] + [to_x(d) for d in (1, 2, 3)] + [to_h(d) for d in (1, 2, 3)]
+    peers += [to_y(d) for d in range(1, NY)]
+    for peer in peers:
+        pl.semaphore_signal(barrier, inc=1, device_id=peer, device_id_type=MESH)
     plan_in = [
         pltpu.make_async_copy(rows_hbm, rows_in, sem_a.at[8]),
         pltpu.make_async_copy(counts_hbm, counts_in, sem_a.at[9]),
@@ -92,11 +97,6 @@
     for cp in loads:
         cp.start()
 
-    barrier = pltpu.get_barrier_semaphore()
-    peers = [sib, mate] + [to_x(d) for d in (1, 2, 3)] + [to_h(d) for d in (1, 2, 3)]
-    peers += [to_y(d) for d in range(1, NY)]
-    for peer in peers:
-        pl.semaphore_signal(barrier, inc=1, device_id=peer, device_id_type=MESH)
     me = node(0, 0, core)
     gt[BR] = jnp.zeros((B, B), BF)
     seg[NB] = jnp.zeros((B, F), F32)
@@ -284,7 +284,6 @@
             w_to_col()
 
     arrived(gt.at[pl.ds(0, NY)], g_r.at[BR])
-    w_to_plane()
     def column_grad(j):
         picked = jnp.concatenate([gt[idx[2, q * NC + j]] for q in range(SLOTS)], axis=1)
         return jnp.dot(picked, adj[j], preferred_element_type=F32)
@@ -318,7 +317,9 @@
             produce(*steps[n])
         if n >= lag:
             pass_on(*steps[n - lag])
-        if n == 10:
+        if n == 3:
+            w_to_plane()
+        if n == 15:
             w_from_plane()
 
     def hcopy(dz):

time: 69.5 us -> 67.7 us (0.974)
  Pallas kernels: 67.5 us -> 65.7 us
    pallas_call x1, Pallas kernels: 67.5 us -> 65.7 us  [body(): pl.pallas_call(kernel, out_shape=(jax.ShapeDtypeStruct((B, F), BF), jax.S...]
where the time goes in v4:
time: 67.7 us; the launch traced here: 67.6 us
  Pallas kernels  65.7 us (97%)
  local copies, waits for them, and re-layouts  1.27 us (2%)
    pallas_call x1, Pallas kernels, body(): pl.pallas_call(kernel, out_shape=(jax.ShapeDtypeStruct((B, F), BF), jax.S...  65.7 us

profile of v4, /device:TPU:1, one launch (start us, length us, event | category | flops | bytes accessed | tf_op | source)
XLA Modules:
  0.0 67.6 jit_solution(9169637035171168620)
XLA Ops:
  0.6 65.7 %shard_map.77 = (bf16[128,128]{1,0:T(8,128)(2,1)S(1)}, f32[128,256]{1,0:T(8,128)S(1)}) custom-call(s32[4,32]{1,0:T(4,128)} %bitcast.5, s32[1,32]{1,0:T(1,128)} %counts_hbm.1, bf16[128,128]{1,0:T(8,128)(2,1)} %emb_hbm.1, bf16[128,256]{1,0:T(8,128)(2,1)} %wgt_hbm.1, bf16[128,256]{1,0:T(8,128)(2,1)} %cot_hbm.1, bf16[32,512,128]{2,1,0:T(8,128)(2,1)} %bitcast.4), custom_call_target="tpu_custom_call" | custom-call | tf_op jit(solution)/shard_map/pallas_call | solution.py:362
  66.3 0.6 copy.10
  66.9 0.7 copy.11

commit v5 on v4

--- a/solution.py
+++ b/solution.py
@@ -190,7 +190,7 @@
         seg[i] = total
         return total
 
-    lax.fori_loop(0, NB, segment, jnp.zeros((B, F), F32))
+    lax.fori_loop(0, NB, segment, jnp.zeros((B, F), F32), unroll=8)
 
     order = (4, 3, 5, 2, 6, 1, 7, 0)
 

time: 67.7 us -> 66.8 us (0.987)
  Pallas kernels: 65.7 us -> 64.7 us
    pallas_call x1, Pallas kernels: 65.7 us -> 64.7 us  [body(): pl.pallas_call(kernel, out_shape=(jax.ShapeDtypeStruct((B, F), BF), jax.S...]
where the time goes in v5:
time: 66.8 us; the launch traced here: 66.6 us
  Pallas kernels  64.7 us (97%)
  local copies, waits for them, and re-layouts  1.27 us (2%)
    pallas_call x1, Pallas kernels, body(): pl.pallas_call(kernel, out_shape=(jax.ShapeDtypeStruct((B, F), BF), jax.S...  64.7 us

profile of v5, /device:TPU:1, one launch (start us, length us, event | category | flops | bytes accessed | tf_op | source)
XLA Modules:
  0.0 66.6 jit_solution(3138015550993798845)
XLA Ops:
  0.6 64.7 %shard_map.77 = (bf16[128,128]{1,0:T(8,128)(2,1)S(1)}, f32[128,256]{1,0:T(8,128)S(1)}) custom-call(s32[4,32]{1,0:T(4,128)} %bitcast.5, s32[1,32]{1,0:T(1,128)} %counts_hbm.1, bf16[128,128]{1,0:T(8,128)(2,1)} %emb_hbm.1, bf16[128,256]{1,0:T(8,128)(2,1)} %wgt_hbm.1, bf16[128,256]{1,0:T(8,128)(2,1)} %cot_hbm.1, bf16[32,512,128]{2,1,0:T(8,128)(2,1)} %bitcast.4), custom_call_target="tpu_custom_call" | custom-call | tf_op jit(solution)/shard_map/pallas_call | solution.py:362
  65.3 0.6 copy.10
  66.0 0.7 copy.11

commit v6 on v5

--- a/solution.py
+++ b/solution.py
@@ -78,8 +78,8 @@
     own_in = pltpu.make_async_copy(emb_hbm, emb, sem_a.at[4])
     own_in.start()
     barrier = pltpu.get_barrier_semaphore()
-    peers = [sib, mate] + [to_x(d) for d in (1, 2, 3)] + [to_h(d) for d in (1, 2, 3)]
-    peers += [to_y(d) for d in range(1, NY)]
+    peers = [to_h(d) for d in (2, 1, 3)] + [to_y(d) for d in (4, 3, 5, 2, 6)]
+    peers += [to_x(d) for d in (2, 1, 3)] + [to_y(d) for d in (1, 7)] + [mate, sib]
     for peer in peers:
         pl.semaphore_signal(barrier, inc=1, device_id=peer, device_id_type=MESH)
     plan_in = [
@@ -190,7 +190,7 @@
         seg[i] = total
         return total
 
-    lax.fori_loop(0, NB, segment, jnp.zeros((B, F), F32), unroll=8)
+    lax.fori_loop(0, NB, segment, jnp.zeros((B, F), F32), unroll=16)
 
     order = (4, 3, 5, 2, 6, 1, 7, 0)
 

time: 66.8 us -> 67.6 us (1.012)
  Pallas kernels: 64.7 us -> 65.6 us
    pallas_call x1, Pallas kernels: 64.7 us -> 65.6 us  [body(): pl.pallas_call(kernel, out_shape=(jax.ShapeDtypeStruct((B, F), BF), jax.S...]
where the time goes in v6:
time: 67.6 us; the launch traced here: 67.5 us
  Pallas kernels  65.6 us (97%)
  local copies, waits for them, and re-layouts  1.27 us (2%)
    pallas_call x1, Pallas kernels, body(): pl.pallas_call(kernel, out_shape=(jax.ShapeDtypeStruct((B, F), BF), jax.S...  65.6 us

profile of v6, /device:TPU:1, one launch (start us, length us, event | category | flops | bytes accessed | tf_op | source)
XLA Modules:
  0.0 67.5 jit_solution(3629889526833787079)
XLA Ops:
  0.6 65.6 %shard_map.77 = (bf16[128,128]{1,0:T(8,128)(2,1)S(1)}, f32[128,256]{1,0:T(8,128)S(1)}) custom-call(s32[4,32]{1,0:T(4,128)} %bitcast.5, s32[1,32]{1,0:T(1,128)} %counts_hbm.1, bf16[128,128]{1,0:T(8,128)(2,1)} %emb_hbm.1, bf16[128,256]{1,0:T(8,128)(2,1)} %wgt_hbm.1, bf16[128,256]{1,0:T(8,128)(2,1)} %cot_hbm.1, bf16[32,512,128]{2,1,0:T(8,128)(2,1)} %bitcast.4), custom_call_target="tpu_custom_call" | custom-call | tf_op jit(solution)/shard_map/pallas_call | solution.py:362
  66.2 0.6 copy.10
  66.9 0.7 copy.11
